TPU v7x, 128 devices: a whole 4x4x4 slice. The times are simulated.
128 devices in a mesh: dp: 8 (over x, y_lo), feat: 16 (over z, y_hi, core).
Axes of the slice: x: 4, y: 4 (y_hi: 2, y_lo: 2; y = y_hi * 2 + y_lo), z: 4, core: 2. Of those that a mesh axis runs over, the one named last changes fastest.
Arguments:
- view_a: float32 [8192, 4096], P('dp', 'feat'), may hold values from -1000 to 1000
- view_b: float32 [8192, 4096], P('dp', 'feat'), may hold values from -1000 to 1000
Outputs:
- grad_a: float32 [8192, 4096], P('dp', 'feat')
- grad_b: float32 [8192, 4096], P('dp', 'feat')
- loss: float32 [], replicated
All inputs are finite; a program needn't handle non-finite values.
Results may differ from a plain program's by a relative error of at most 0.0017.
Values may be sent and summed in bfloat16 or wider, within the bound.
A program may use at most 128 MiB of HBM per device.

v0:
```python
import jax
import jax.numpy as jnp
from jax import lax
from jax.sharding import PartitionSpec as P

D = 4096


off_weight = 0.0051
variance_eps = 1e-05


def backward(upstream, normed, spread, first, second, batch_size):
    return (upstream - first / batch_size - normed * (second / batch_size)) / spread


def per_device(view_a, view_b):
    row_count = view_a.shape[0]
    batch_size = row_count * lax.axis_size("dp")
    sum_a, sum_b = lax.psum((jnp.sum(view_a, axis=0), jnp.sum(view_b, axis=0)), "dp")
    shifted_a = view_a - sum_a / batch_size
    shifted_b = view_b - sum_b / batch_size
    square_a, square_b = lax.psum(
        (jnp.sum(shifted_a * shifted_a, axis=0), jnp.sum(shifted_b * shifted_b, axis=0)), "dp"
    )
    variance_a = square_a / batch_size
    variance_b = square_b / batch_size
    spread_a = jnp.sqrt(variance_a + variance_eps)
    spread_b = jnp.sqrt(variance_b + variance_eps)
    normed_a = shifted_a / spread_a
    normed_b = shifted_b / spread_b
    half_a = normed_a.astype(jnp.bfloat16)
    half_b = normed_b.astype(jnp.bfloat16)
    whole_b = lax.all_gather(half_b, "feat", axis=1, tiled=True)
    partial_block = lax.dot_general(
        half_a, whole_b, (((0,), (0,)), ((), ())), preferred_element_type=jnp.float32
    )
    correlation = lax.psum(partial_block, "dp") / batch_size
    local_width = half_a.shape[1]
    first_column = lax.axis_index("feat") * local_width
    row_ids = lax.broadcasted_iota(jnp.int32, correlation.shape, 0) + first_column
    column_ids = lax.broadcasted_iota(jnp.int32, correlation.shape, 1)
    on_diagonal = row_ids == column_ids
    diagonal = jnp.sum(jnp.where(on_diagonal, correlation, 0.0), axis=1)
    local_loss = jnp.sum((1.0 - diagonal) ** 2) + off_weight * (
        jnp.sum(correlation * correlation) - jnp.sum(diagonal * diagonal)
    )
    total_loss = lax.psum(local_loss, "feat") / D
    weights = jnp.where(
        on_diagonal, -2.0 * (1.0 - correlation), 2.0 * off_weight * correlation
    ).astype(jnp.bfloat16)
    upstream_a = lax.dot_general(
        whole_b, weights, (((1,), (1,)), ((), ())), preferred_element_type=jnp.float32
    )
    terms = jnp.dot(half_a, weights, preferred_element_type=jnp.float32)
    upstream_b = lax.psum_scatter(terms, "feat", scatter_dimension=1, tiled=True)
    first_a, second_a, first_b, second_b = lax.psum(
        (
            jnp.sum(upstream_a, axis=0),
            jnp.sum(upstream_a * normed_a, axis=0),
            jnp.sum(upstream_b, axis=0),
            jnp.sum(upstream_b * normed_b, axis=0),
        ),
        "dp",
    )
    grad_a = backward(upstream_a, normed_a, spread_a, first_a, second_a, batch_size)
    grad_b = backward(upstream_b, normed_b, spread_b, first_b, second_b, batch_size)
    return (grad_a, grad_b, total_loss)


def solution(mesh):
    in_specs = (P("dp", "feat"), P("dp", "feat"))
    out_specs = (P("dp", "feat"), P("dp", "feat"), P())
    return jax.shard_map(
        per_device, mesh=mesh, in_specs=in_specs, out_specs=out_specs, check_vma=False
    )
```

profile of v0, /device:TPU:0, one launch (start us, length us, event | category | flops | bytes accessed | tf_op | source)
XLA Modules:
  0.0 506.2 jit_solution(14392374726666496956)
XLA Ops:
  7.2 0.0 all-gather.2.cloned.1.call-start
  7.2 1.5 reduce_sum.108
  8.7 1.4 reduce_sum.110
  10.1 19.8 %all-reduce.2 = (f32[256]{0:T(256)S(1)}, f32[256]{0:T(256)S(1)}) all-reduce(f32[256]{0:T(256)S(1)} %reduce_sum.108, f32[256]{0:T(256)S(1)} %reduce_sum.110), channel_id=1, replica_groups=mesh['dp'=8,'feat'=16] {'dp'}, use_global_device_ids=true, to_apply=%region_1.0 | all-reduce | flops 512 | bytes 4096 | tf_op jit(solution)/shard_map/psum | solution.py:20
  29.9 1.4 multiply_reduce_fusion.4
  31.3 1.4 multiply_reduce_fusion.3
  32.7 15.9 %all-reduce.1 = (f32[256]{0:T(256)S(1)}, f32[256]{0:T(256)S(1)}) all-reduce(f32[256]{0:T(256)S(1)} %multiply_reduce_fusion.4, f32[256]{0:T(256)S(1)} %multiply_reduce_fusion.3), channel_id=1, replica_groups=mesh['dp'=8,'feat'=16] {'dp'}, use_global_device_ids=true, to_apply=%region_3.0 | all-reduce | flops 512 | bytes 4096 | tf_op jit(solution)/shard_map/psum | solution.py:23
  48.7 0.9 fusion.4
  49.6 0.0 all-gather.2.cloned.1.call-update
  49.6 0.0 all-reduce.5.cloned.1.call-start
  49.7 77.5 %all-gather.2.cloned.1.call-done = bf16[1024,4096]{1,0:T(8,128)(2,1)} async-done(((bf16[1024,256]{1,0:T(8,128)(2,1)}), bf16[1024,4096]{1,0:T(8,128)(2,1)}) %all-gather.2.cloned.1.call-update) | async-done | bytes 8388624 | tf_op jit(solution)/shard_map/all_gather | solution.py:34
  127.2 7.7 %fusion.2 = f32[256,4096]{1,0:T(8,128)} fusion(bf16[1024,4096]{1,0:T(8,128)(2,1)} %all-gather.2.cloned.1.call-done, f32[1024,256]{1,0:T(8,128)S(1)} %copy-done, f32[256]{0:T(256)S(1)} %add_sqrt_fusion, f32[256]{0:T(256)S(1)} %get-tuple-element.20), kind=kOutput, calls=%fused_computation.14 | convolution fusion | flops 2148270080 | bytes 13633536 | tf_op jit(solution)/shard_map/dot_general | solution.py:35
  134.9 0.0 reduce-scatter.2.cloned.1.call-start
  135.0 179.3 %all-reduce.5.cloned.1.call-done = f32[256,4096]{1,0:T(8,128)} async-done(((f32[256,4096]{1,0:T(8,128)}), f32[256,4096]{1,0:T(8,128)}) %all-reduce.5.cloned.1.call-update) | async-done | bytes 4194320 | tf_op jit(solution)/shard_map/psum | solution.py:38
  314.3 10.6 %fusion = f32[1024,4096]{1,0:T(8,128)} fusion(f32[1024,256]{1,0:T(8,128)S(1)} %copy-done, f32[256]{0:T(256)S(1)} %add_sqrt_fusion, f32[256]{0:T(256)S(1)} %get-tuple-element.20, f32[256,4096]{1,0:T(8,128)} %all-reduce.5.cloned.1.call-done, s32[256]{0:T(256)S(1)} %iota_add_fusion), kind=kOutput, calls=%fused_computation.12 | convolution fusion | flops 2155610112 | bytes 22023168 | tf_op jit(solution)/shard_map/dot_general | solution.py:55
  324.9 4.6 multiply_reduce_fusion
  329.5 0.6 multiply_reduce_fusion.5
  332.1 38.1 %psum.79 = f32[]{:T(128)} all-reduce(f32[]{:T(128)S(6)} %add.42), channel_id=1, replica_groups=mesh['dp'=8,'feat'=16] {'feat'}, use_global_device_ids=true, to_apply=%region_22.23 | all-reduce | flops 1 | bytes 8 | tf_op jit(solution)/shard_map/psum | solution.py:48
  370.8 8.2 %fusion.7 = (f32[256]{0:T(256)S(1)}, f32[256]{0:T(256)S(1)}, f32[1024,256]{1,0:T(8,128)}) fusion(f32[256]{0:T(256)S(1)} %add_sqrt_fusion, f32[1024,256]{1,0:T(8,128)S(1)} %copy-done, f32[256]{0:T(256)S(1)} %get-tuple-element.20, bf16[1024,4096]{1,0:T(8,128)(2,1)} %all-gather.2.cloned.1.call-done, f32[256,4096]{1,0:T(8,128)} %all-reduce.5.cloned.1.call-done, ...), kind=kOutput, calls=%fused_computation.30 | convolution fusion | flops 2156133888 | bytes 14685184 | tf_op jit(solution)/shard_map/dot_general | solution.py:52
  378.9 95.8 %reduce-scatter.2.cloned.1.call-done = f32[1024,256]{1,0:T(8,128)} async-done(((f32[1024,4096]{1,0:T(8,128)}), f32[1024,256]{1,0:T(8,128)}) %reduce-scatter.2.cloned.1.call-update) | async-done | bytes 1048592 | tf_op jit(solution)/shard_map/reduce_scatter | solution.py:56
  474.7 1.5 fusion.6
  476.3 18.7 %all-reduce = (f32[256]{0:T(256)S(1)}, f32[256]{0:T(256)S(1)}, f32[256]{0:T(256)S(1)}, f32[256]{0:T(256)S(1)}) all-reduce(f32[256]{0:T(256)S(1)} %get-tuple-element.8, f32[256]{0:T(256)S(1)} %get-tuple-element.7, f32[256]{0:T(256)S(1)} %get-tuple-element.6, f32[256]{0:T(256)S(1)} %get-tuple-element.5), channel_id=1, replica_groups=mesh['dp'=8,'feat'=16] {'dp'}, use_global_device_ids=true, to_apply=%region_12.13 | all-reduce | flops 1024 | bytes 8192 | tf_op jit(solution)/shard_map/psum | solution.py:57
  495.0 2.4 subtract_divide_fusion.1
  497.4 1.2 subtract_divide_fusion
  (16 shorter events, 0.1 us)
Async XLA Ops:
  7.2 41.5 %copy-start.1 = (f32[1024,256]{1,0:T(8,128)S(1)}, f32[1024,256]{1,0:T(8,128)}, u32[]{:S(2)}) copy-start(f32[1024,256]{1,0:T(8,128)} %param.3) | copy-start | bytes 3145732
  7.2 120.0 %copy-start = (f32[1024,256]{1,0:T(8,128)S(1)}, f32[1024,256]{1,0:T(8,128)}, u32[]{:S(2)}) copy-start(f32[1024,256]{1,0:T(8,128)} %param.2) | copy-start | bytes 3145732
  7.2 120.0 %all-gather.2.cloned.1.call-start = ((), (), s32[]{:S(2)}) async-start(), calls=%async_computation.1 | async-start | bytes 8912896 | tf_op jit(solution)/shard_map/all_gather | solution.py:34
  49.6 264.7 %all-reduce.5.cloned.1.call-start = ((), (), s32[]{:S(2)}) async-start(), calls=%async_computation.2 | async-start | bytes 8388608 | tf_op jit(solution)/shard_map/psum | solution.py:38
  134.9 339.8 %reduce-scatter.2.cloned.1.call-start = ((), (), s32[]{:S(2)}) async-start(), calls=%async_computation.3 | async-start | bytes 17825792 | tf_op jit(solution)/shard_map/reduce_scatter | solution.py:56
  474.7 22.7 %copy-start.2 = (f32[1024,256]{1,0:T(8,128)S(1)}, f32[1024,256]{1,0:T(8,128)}, u32[]{:S(2)}) copy-start(f32[1024,256]{1,0:T(8,128)} %reduce-scatter.2.cloned.1.call-done) | copy-start | bytes 3145732
Sparse Core Ops, SparseCore 0:
  49.7 77.4 all-gather.1
  135.1 179.2 all-reduce.4
  325.0 149.6 reduce-scatter.1
where the time goes:
time: 507 us; the launch traced here: 506 us
  waiting for transfers between devices  353 us (70%)
  blocking collectives  92.5 us (18%)
  matrix products  26.5 us (5%)
  between operations  17.5 us (3%)
  other arithmetic  16.9 us (3%)
    psum x1, waiting for transfers between devices, per_device(): correlation = lax.psum(partial_block, 'dp') / batch_size  179 us
    reduce_scatter x1, waiting for transfers between devices, per_device(): lax.psum_scatter(terms, 'feat', scatter_dimension=1, tiled=True)  95.8 us
    all_gather x1, waiting for transfers between devices, per_device(): whole_b = lax.all_gather(half_b, 'feat', axis=1, tiled=True)  77.5 us
    psum x1, blocking collectives, per_device(): total_loss = lax.psum(local_loss, 'feat') / D  38.1 us
    psum x1, blocking collectives, per_device(): lax.psum((jnp.sum(view_a, axis=0), jnp.sum(view_b, axis=0)), 'dp')  19.8 us
    psum x1, blocking collectives, per_device(): lax.psum((jnp.sum(upstream_a, axis=0), jnp.sum(upstream_a * normed_a, axi...  18.7 us
    psum x1, blocking collectives, per_device(): lax.psum((jnp.sum(shifted_a * shifted_a, axis=0), jnp.sum(shifted_b * shi...  15.9 us
    dot_general x1, matrix products, per_device(): terms = jnp.dot(half_a, weights, preferred_element_type=jnp.float32)  10.6 us
  transfers between devices with their start and end apart: 3, of which 3 were waited for; matrix products, arithmetic and copies ran while one was open for 3% of the time, Pallas kernels for 0%

commit v1 on v0

v1 whole, which is shorter than its diff:
```python
import functools

import jax
import jax.numpy as jnp
from jax import lax
from jax.experimental import pallas as pl
from jax.experimental.pallas import tpu as pltpu
from jax.sharding import PartitionSpec as P

D = 4096
BATCH = 8192
ROWS = 1024
COLS = 256
WIDE = 4 * COLS
EXTRA = 16
OWNED = COLS // 8

off_weight = 0.0051
variance_eps = 1e-05
scale_off = 2.0 * off_weight / BATCH

MESH = pl.DeviceIdType.MESH
BF16 = jnp.bfloat16
F32 = jnp.float32
VMEM = pltpu.VMEM
DMA = pltpu.SemaphoreType.DMA


def flip(index, mask):
    for bit in (1, 2, 4, 8):
        if mask & bit:
            index = index + bit - 2 * bit * ((index // bit) % 2)
    return index


def tree_sum(terms):
    while len(terms) > 1:
        terms = [terms[i] + terms[i + 1] for i in range(0, len(terms), 2)]
    return terms[0]


def matmul(a, b, contract):
    return lax.dot_general(a, b, (contract, ((), ())), preferred_element_type=F32)


def column_sum(value):
    return jnp.sum(value, axis=0, keepdims=True)


def kernel(
    va, vb, ga, gb, loss,
    stat, mid, sums_a, sums_b, vec_a, vec_b, vec_l,
    a_buf, b_buf, bt, corr, c_send, c_recv, w_buf,
    ua_acc, ub_own, ua_near, ua_send, ua_recv, ub_send, ub_recv, second_acc,
    stat_s, stat_r, mid_s, mid_r, sum_s, sum_r, vec_s, vec_r, vl_s, vl_r,
    a_s, a_r, b_s, b_r, c_s, c_r, w_s, w_r, ua_s, ua_r, ub_s, ub_r,
):
    p = lax.axis_index("dp")
    f = lax.axis_index("feat")
    dp_peer = [(flip(p, r), f) for r in range(8)]
    j_peer = [(p, flip(f, r)) for r in range(4)]
    z_peer = [(p, flip(f, 4 * r)) for r in range(4)]
    pending = []

    def copy(src, dst, send_sem, recv_sem, peer):
        return pltpu.make_async_remote_copy(
            src_ref=src, dst_ref=dst, send_sem=send_sem, recv_sem=recv_sem,
            device_id=peer, device_id_type=MESH,
        )

    def start(*args):
        handle = copy(*args)
        handle.start()
        pending.append(handle)
        return handle

    barrier = pltpu.get_barrier_semaphore()
    for peer in dp_peer[1:] + j_peer[1:] + z_peer[1:]:
        pl.semaphore_signal(barrier, inc=1, device_id=peer, device_id_type=MESH)

    zero_row = jnp.zeros((1, COLS), F32)
    mean_a = column_sum(va[...]) / ROWS
    mean_b = column_sum(vb[...]) / ROWS
    square_a = column_sum((va[...] - mean_a) ** 2)
    square_b = column_sum((vb[...] - mean_b) ** 2)
    stat[0] = jnp.concatenate([mean_a, square_a, mean_b, square_b] + [zero_row] * 4, axis=0)
    pl.semaphore_wait(barrier, 13)
    arrive = [start(stat.at[0], stat.at[r], stat_s.at[r], stat_r.at[r], dp_peer[r]) for r in range(1, 8)]
    for handle in arrive:
        handle.wait_recv()
    every = [stat[r] for r in range(8)]
    mean = tree_sum(every) / 8
    spreads = tree_sum([(t - mean) ** 2 for t in every]) * ROWS
    squares = tree_sum(every)
    center_a, center_b = mean[0:1], mean[2:3]
    spread_a = jnp.sqrt((squares[1:2] + spreads[0:1]) / BATCH + variance_eps)
    spread_b = jnp.sqrt((squares[3:4] + spreads[2:3]) / BATCH + variance_eps)
    inverse_a, inverse_b = 1.0 / spread_a, 1.0 / spread_b

    b_buf[0, 0:ROWS] = ((vb[...] - center_b) * inverse_b).astype(BF16)
    b_near = [
        start(b_buf.at[0, pl.ds(0, ROWS)], b_buf.at[r, pl.ds(0, ROWS)], b_s.at[r], b_r.at[r], z_peer[r])
        for r in (1, 3)
    ]
    pending = pending[:-2]
    a_buf[0, 0:ROWS] = ((va[...] - center_a) * inverse_a).astype(BF16)
    a_near = [start(a_buf.at[0, pl.ds(0, ROWS)], a_buf.at[r, pl.ds(0, ROWS)], a_s.at[r], a_r.at[r], j_peer[r]) for r in (2, 1)]
    half_a = a_buf[0, 0:ROWS].astype(F32)
    half_b = b_buf[0, 0:ROWS].astype(F32)
    mid[0] = jnp.concatenate(
        [column_sum(half_a * half_b), column_sum(half_a), column_sum(half_b)] + [zero_row] * 5, axis=0
    )
    mid_arrive = [start(mid.at[0], mid.at[r], mid_s.at[r], mid_r.at[r], dp_peer[r]) for r in range(1, 8)]
    bt[...] = b_buf[0, 0:ROWS].T
    for handle in mid_arrive:
        handle.wait_recv()
    totals = tree_sum([mid[r] for r in range(8)])
    sums_a[0] = totals
    sums_b[0] = totals
    sum_arrive = [start(sums_a.at[0], sums_a.at[r], sum_s.at[r], sum_r.at[r], j_peer[r]) for r in range(1, 4)]
    sum_arrive += [start(sums_b.at[0], sums_b.at[r], sum_s.at[3 + r], sum_r.at[3 + r], z_peer[r]) for r in range(1, 4)]
    diagonal = totals[0:1] / BATCH
    diag_weight = (-2.0 * (1.0 - diagonal)).astype(BF16).astype(F32)

    def correlate(k, m):
        block = matmul(bt[...], a_buf[m, 0:ROWS], ((1,), (0,)))
        if k == 0 and m == 0:
            same = lax.broadcasted_iota(jnp.int32, block.shape, 0) == lax.broadcasted_iota(jnp.int32, block.shape, 1)
            block = jnp.where(same, 0.0, block)
        corr[k, :, m * COLS : (m + 1) * COLS] = block
        c_send[k, :, m * COLS : (m + 1) * COLS] = block.astype(BF16)

    def scatter(k):
        got = []
        for r in range(1, 8):
            rows = pl.ds(pl.multiple_of(dp_peer[r][0] * OWNED, OWNED), OWNED)
            got.append(start(c_send.at[k, rows], c_recv.at[k, r], c_s.at[k, r], c_r.at[k, r], dp_peer[r]))
        return got

    own_rows = pl.ds(pl.multiple_of(p * OWNED, OWNED), OWNED)

    def reduce(k, got):
        for handle in got:
            handle.wait_recv()
        total = tree_sum([corr[k, own_rows, :]] + [c_recv[k, r].astype(F32) for r in range(1, 8)])
        w_buf[k, own_rows, :] = (total * scale_off).astype(BF16)
        part = w_buf.at[k, own_rows]
        return [start(part, part, w_s.at[k, r], w_r.at[k, r], dp_peer[r]) for r in range(1, 8)]

    correlate(0, 0)
    a_near[1].wait_recv()
    correlate(0, 1)
    a_near[0].wait_recv()
    a_far = start(a_buf.at[2, pl.ds(0, ROWS)], a_buf.at[3, pl.ds(0, ROWS)], a_s.at[3], a_r.at[3], j_peer[1])
    correlate(0, 2)
    a_far.wait_recv()
    correlate(0, 3)
    parts = {0: scatter(0)}
    for handle in b_near:
        handle.wait_send()
    b_far = start(b_buf.at[0, pl.ds(0, ROWS)], b_buf.at[2, pl.ds(0, ROWS)], b_s.at[2], b_r.at[2], z_peer[2])
    weights = {}
    for k, handle in ((1, b_near[0]), (3, b_near[1]), (2, b_far)):
        handle.wait_recv()
        bt[...] = b_buf[k, 0:ROWS].T
        for m in range(4):
            correlate(k, m)
        parts[k] = scatter(k)
        if k == 3:
            weights[0] = reduce(0, parts[0])
    for handle in sum_arrive:
        handle.wait_recv()
    for r in range(4):
        for sums, row, buf in ((sums_a, 1, a_buf), (sums_b, 2, b_buf)):
            value = sums[r, row : row + 1]
            high = value.astype(BF16)
            low = (value - high.astype(F32)).astype(BF16)
            buf[r, ROWS : ROWS + EXTRA] = jnp.concatenate(
                [high.astype(F32), low.astype(F32), jnp.zeros((EXTRA - 2, COLS), F32)], axis=0
            ).astype(BF16)
    for k in (1, 3, 2):
        weights[k] = reduce(k, parts[k])

    ub_arrive = {}
    vecb_arrive = {}
    for n, k in enumerate((0, 1, 3, 2)):
        for handle in weights[k]:
            handle.wait_recv()
        total = None
        for m in range(4):
            w = w_buf[k, :, m * COLS : (m + 1) * COLS]
            term = matmul(a_buf[m], w, ((1,), (1,)))
            total = term if total is None else total + term
        if k == 0:
            ub_own[...] = total[0:ROWS]
        else:
            ub_send[k] = total[0:ROWS].astype(BF16)
            ub_arrive[k] = start(ub_send.at[k], ub_recv.at[k], ub_s.at[k], ub_r.at[k], z_peer[k])
        square = jnp.square(w_buf[k].astype(F32))
        over_second = column_sum(square)
        folded = sum(square[:, i * 128 : (i + 1) * 128] for i in range(8))
        over_first = column_sum(folded.T)
        first = total[ROWS : ROWS + 1] + total[ROWS + 1 : ROWS + 2]
        slot = vec_b.at[0 if k == 0 else 3 + k]
        slot[...] = jnp.concatenate([first, over_first] + [zero_row] * 6, axis=0)
        if k:
            vecb_arrive[k] = start(slot, vec_b.at[k], vec_s.at[3 + k], vec_r.at[3 + k], z_peer[k])
        if n == 0:
            second_acc[0:1] = over_second
        else:
            second_acc[0:1] += over_second
        for m in range(4):
            w = w_buf[k, :, m * COLS : (m + 1) * COLS]
            term = matmul(b_buf[k], w, ((1,), (0,)))
            if n == 0:
                ua_acc[m] = term
            else:
                ua_acc[m] += term
    ua3 = start(ua_acc.at[3, pl.ds(0, ROWS)], ua_near.at[1], ua_s.at[3], ua_r.at[3], j_peer[1])
    ua1 = start(ua_acc.at[1, pl.ds(0, ROWS)], ua_near.at[0], ua_s.at[1], ua_r.at[1], j_peer[1])

    block_sum = sum(second_acc[0:1, m * COLS : (m + 1) * COLS] for m in range(4))
    loss_row = (1.0 - diagonal) ** 2 + (0.25 / off_weight) * block_sum
    vec_arrive = []
    for r in range(4):
        first = ua_acc[r, ROWS : ROWS + 1] + ua_acc[r, ROWS + 1 : ROWS + 2]
        second = second_acc[0:1, r * COLS : (r + 1) * COLS]
        slot = vec_a.at[0 if r == 0 else 3 + r]
        slot[...] = jnp.concatenate([first, second, loss_row] + [zero_row] * 5, axis=0)
        if r:
            vec_arrive.append(start(slot, vec_a.at[r], vec_s.at[r], vec_r.at[r], j_peer[r]))
    ua3.wait_recv()
    ua_send[...] = (ua_acc[2, 0:ROWS] + ua_near[1]).astype(BF16)
    ua2 = start(ua_send, ua_recv, ua_s.at[2], ua_r.at[2], j_peer[2])
    for handle in vec_arrive:
        handle.wait_recv()
    sum_a = tree_sum([vec_a[r] for r in range(4)])
    vec_l[0] = sum_a
    loss_arrive = [start(vec_l.at[0], vec_l.at[r], vl_s.at[r], vl_r.at[r], z_peer[r]) for r in range(1, 4)]
    for handle in vecb_arrive.values():
        handle.wait_recv()
    sum_b = tree_sum([vec_b[r] for r in range(4)])
    for handle in loss_arrive:
        handle.wait_recv()
    losses = tree_sum([vec_l[r] for r in range(4)])
    loss[...] = jnp.sum(losses[2:3], axis=1, keepdims=True) / D

    def finish(upstream, view, center, inverse, own_sum, sums, out):
        first = (sums[0:1] + diag_weight * own_sum) / BATCH
        second = sums[1:2] * (0.5 / off_weight) + diag_weight * diagonal
        normed = (view[...] - center) * inverse
        out[...] = (upstream - first - normed * second) * inverse

    for k in (1, 3, 2):
        ub_arrive[k].wait_recv()
    upstream_b = ub_own[...] + sum(ub_recv[k].astype(F32) for k in (1, 2, 3)) + diag_weight * a_buf[0, 0:ROWS].astype(F32)
    finish(upstream_b, vb, center_b, inverse_b, totals[1:2], sum_b, gb)
    ua1.wait_recv()
    ua2.wait_recv()
    upstream_a = ua_acc[0, 0:ROWS] + ua_near[0] + ua_recv[...].astype(F32) + diag_weight * b_buf[0, 0:ROWS].astype(F32)
    finish(upstream_a, va, center_a, inverse_a, totals[2:3], sum_a, ga)

    for handle in pending:
        handle.wait_send()


def per_device(view_a, view_b):
    small = VMEM((8, 8, COLS), F32)
    block = VMEM((4, ROWS + EXTRA, COLS), BF16)
    plain = VMEM((4, ROWS, COLS), BF16)
    chunk = (4, COLS, WIDE)
    grad_a, grad_b, loss = pl.pallas_call(
        kernel,
        out_shape=(
            jax.ShapeDtypeStruct((ROWS, COLS), F32),
            jax.ShapeDtypeStruct((ROWS, COLS), F32),
            jax.ShapeDtypeStruct((1, 1), F32),
        ),
        in_specs=[pl.BlockSpec(memory_space=VMEM)] * 2,
        out_specs=[pl.BlockSpec(memory_space=VMEM)] * 3,
        scratch_shapes=[
            small, small, small, small, small, small, small,
            block, block, VMEM((COLS, ROWS), BF16), VMEM(chunk, F32), VMEM(chunk, BF16),
            VMEM((4, 8, OWNED, WIDE), BF16), VMEM(chunk, BF16),
            VMEM((4, ROWS + EXTRA, COLS), F32), VMEM((ROWS, COLS), F32),
            VMEM((2, ROWS, COLS), F32), VMEM((ROWS, COLS), BF16), VMEM((ROWS, COLS), BF16), plain, plain, VMEM((8, WIDE), F32),
            DMA((8,)), DMA((8,)), DMA((8,)), DMA((8,)), DMA((8,)), DMA((8,)), DMA((8,)), DMA((8,)), DMA((4,)), DMA((4,)),
            DMA((4,)), DMA((4,)), DMA((4,)), DMA((4,)), DMA((4, 8)), DMA((4, 8)), DMA((4, 8)), DMA((4, 8)),
            DMA((4,)), DMA((4,)), DMA((4,)), DMA((4,)),
        ],
        compiler_params=pltpu.CompilerParams(
            collective_id=0, has_side_effects=True, vmem_limit_bytes=56 * 1024 * 1024
        ),
        cost_estimate=pl.CostEstimate(flops=3 * 2 * 1024**3, bytes_accessed=4 * 1024 * 1024, transcendentals=0),
        name="twins",
    )(view_a, view_b)
    return grad_a, grad_b, loss[0, 0]


def solution(mesh):
    in_specs = (P("dp", "feat"), P("dp", "feat"))
    out_specs = (P("dp", "feat"), P("dp", "feat"), P())
    return jax.shard_map(
        per_device, mesh=mesh, in_specs=in_specs, out_specs=out_specs, check_vma=False
    )
```

time: 507 us -> 109 us (0.21)
  waiting for transfers between devices: 353 us -> 0 us
  Pallas kernels: 0 us -> 101 us
  blocking collectives: 92.5 us -> 0 us
  matrix products: 26.5 us -> 0 us
  other arithmetic: 16.9 us -> 0 us
  between operations: 17.5 us -> 2.39 us
    psum x1 -> x0, waiting for transfers between devices: 179 us -> none  [per_device(): correlation = lax.psum(partial_block, 'dp') / batch_size]
    pallas_call x0 -> x1, Pallas kernels: none -> 101 us  [per_device(): pl.pallas_call(kernel, out_shape=(jax.ShapeDtypeStruct((ROWS, COLS), F32)...]
    reduce_scatter x1 -> x0, waiting for transfers between devices: 95.8 us -> none  [per_device(): lax.psum_scatter(terms, 'feat', scatter_dimension=1, tiled=True)]
    psum x4 -> x0, blocking collectives: 92.5 us -> none  [the longest x1 38.1 us: per_device(): total_loss = lax.psum(local_loss, 'feat') / D]
    all_gather x1 -> x0, waiting for transfers between devices: 77.5 us -> none  [per_device(): whole_b = lax.all_gather(half_b, 'feat', axis=1, tiled=True)]
    dot_general x3 -> x0, matrix products: 26.5 us -> none  [the longest x1 10.6 us: per_device(): terms = jnp.dot(half_a, weights, preferred_element_type=jnp.float32)]
    reduce_sum x7 -> x0, other arithmetic: 12.4 us -> none  [the longest x1 4.57 us: per_device(): jnp.sum(correlation * correlation) - jnp.sum(diagonal * diagonal)]
  transfers between devices with their start and end apart: 3 -> 0, of which waited for: 3 -> 0; matrix products, arithmetic and copies ran while one was open for 3% -> 0% of each run, Pallas kernels for 0% -> 0%
where the time goes in v1:
time: 109 us; the launch traced here: 107 us
  Pallas kernels  101 us (93%)
  local copies, waits for them, and re-layouts  3.32 us (3%)
  between operations  2.39 us (2%)
    pallas_call x1, Pallas kernels, per_device(): pl.pallas_call(kernel, out_shape=(jax.ShapeDtypeStruct((ROWS, COLS), F32)...  101 us
    unnamed x4, local copies, waits for them, and re-layouts  3.32 us

profile of v1, /device:TPU:0, one launch (start us, length us, event | category | flops | bytes accessed | tf_op | source)
XLA Modules:
  0.0 107.0 jit_solution(17441395919155078286)
XLA Ops:
  0.6 101.3 %twins.1 = (f32[1024,256]{1,0:T(8,128)}, f32[1024,256]{1,0:T(8,128)}, f32[1,1]{1,0:T(1,128)}) custom-call(f32[1024,256]{1,0:T(8,128)} %va.1, f32[1024,256]{1,0:T(8,128)} %vb.1), custom_call_target="tpu_custom_call" | custom-call | flops 6442450944 | bytes 4194304 | tf_op jit(solution)/shard_map/twins/pallas_call | solution.py:272
  101.9 0.0 copy-start
  101.9 2.4 %copy.8 = f32[1024,256]{1,0:T(8,128)} copy(f32[1024,256]{1,0:T(8,128)} %get-tuple-element.12) | data formatting | bytes 2097152
  104.3 0.0 copy-done
  104.3 1.0 copy.9
Async XLA Ops:
  101.9 2.4 %copy-start = (f32[1024,256]{1,0:T(8,128)S(1)}, f32[1024,256]{1,0:T(8,128)}, u32[]{:S(2)}) copy-start(f32[1024,256]{1,0:T(8,128)} %get-tuple-element.13) | copy-start | bytes 3145732

commit v2 on v1

v2 whole, which is shorter than its diff:
```python
import functools

import jax
import jax.numpy as jnp
from jax import lax
from jax.experimental import pallas as pl
from jax.experimental.pallas import tpu as pltpu
from jax.sharding import PartitionSpec as P

D = 4096
BATCH = 8192
ROWS = 1024
COLS = 256
WIDE = 4 * COLS
EXTRA = 16
OWNED = COLS // 8

off_weight = 0.0051
variance_eps = 1e-05
scale_off = 2.0 * off_weight / BATCH
along = 0.5 / off_weight

MESH = pl.DeviceIdType.MESH
BF16 = jnp.bfloat16
F32 = jnp.float32
VMEM = pltpu.VMEM
DMA = pltpu.SemaphoreType.DMA


def flip(index, mask):
    for bit in (1, 2, 4, 8):
        if mask & bit:
            index = index + bit - 2 * bit * ((index // bit) % 2)
    return index


def tree_sum(terms):
    while len(terms) > 1:
        terms = [terms[i] + terms[i + 1] for i in range(0, len(terms), 2)]
    return terms[0]


def matmul(a, b, contract):
    return lax.dot_general(a, b, (contract, ((), ())), preferred_element_type=F32)


def column_sum(value):
    return jnp.sum(value, axis=0, keepdims=True)


def kernel(
    va_hbm, vb_hbm, ga, gb, loss,
    va, vb,
    stat, mid, sums_a, sums_b, vec_a, vec_b, vec_l,
    coef_j, coef_z, a_raw, b_raw, a_buf, b_buf, bt, corr, c_send, c_relay, c_right, c_left, c_cross, w_buf,
    ua_acc, ub_own, ua_near, ua_send, ua_recv, ub_send, ub_recv, second_acc,
    io, stat_s, stat_r, mid_s, mid_r, sum_s, sum_r, vec_s, vec_r, vl_s, vl_r,
    coef_s, coef_r, a_s, a_r, b_s, b_r, c_s, c_r, w_s, w_r, ua_s, ua_r, ub_s, ub_r,
):
    p = lax.axis_index("dp")
    f = lax.axis_index("feat")
    across = p // 2
    side = p % 2
    dp_peer = [(flip(p, r), f) for r in range(8)]
    j_peer = [(p, flip(f, r)) for r in range(4)]
    z_peer = [(p, flip(f, 4 * r)) for r in range(4)]
    pending = []

    def start(src, dst, send_sem, recv_sem, peer):
        handle = pltpu.make_async_remote_copy(
            src_ref=src, dst_ref=dst, send_sem=send_sem, recv_sem=recv_sem,
            device_id=peer, device_id_type=MESH,
        )
        handle.start()
        pending.append(handle)
        return handle

    barrier = pltpu.get_barrier_semaphore()
    for peer in dp_peer[1:] + j_peer[1:] + z_peer[1:]:
        pl.semaphore_signal(barrier, inc=1, device_id=peer, device_id_type=MESH)
    load_a = pltpu.make_async_copy(va_hbm, va, io.at[0])
    load_b = pltpu.make_async_copy(vb_hbm, vb, io.at[1])
    load_a.start()
    load_b.start()

    zero_row = jnp.zeros((1, COLS), F32)
    load_a.wait()
    mean_a = column_sum(va[...]) / ROWS
    square_a = column_sum((va[...] - mean_a) ** 2)
    load_b.wait()
    mean_b = column_sum(vb[...]) / ROWS
    square_b = column_sum((vb[...] - mean_b) ** 2)
    stat[0] = jnp.concatenate([mean_a, square_a, mean_b, square_b] + [zero_row] * 4, axis=0)
    local_a = jnp.sqrt(square_a / ROWS + variance_eps)
    local_b = jnp.sqrt(square_b / ROWS + variance_eps)
    whole = pl.ds(0, ROWS)
    a_raw[0] = ((va[...] - mean_a) * (1.0 / local_a)).astype(BF16)
    b_raw[0] = ((vb[...] - mean_b) * (1.0 / local_b)).astype(BF16)
    pl.semaphore_wait(barrier, 13)
    arrive = [start(stat.at[0], stat.at[r], stat_s.at[r], stat_r.at[r], dp_peer[r]) for r in range(1, 8)]
    b_near = {r: start(b_raw.at[0], b_raw.at[r], b_s.at[r], b_r.at[r], z_peer[r]) for r in (1, 3)}
    a_near = {r: start(a_raw.at[0], a_raw.at[r], a_s.at[r], a_r.at[r], j_peer[r]) for r in (1, 2)}
    for handle in arrive:
        handle.wait_recv()
    every = [stat[r] for r in range(8)]
    mean = tree_sum(every) / 8
    spreads = tree_sum([(t - mean) ** 2 for t in every]) * ROWS
    squares = tree_sum(every)
    center_a, center_b = mean[0:1], mean[2:3]
    spread_a = jnp.sqrt((squares[1:2] + spreads[0:1]) / BATCH + variance_eps)
    spread_b = jnp.sqrt((squares[3:4] + spreads[2:3]) / BATCH + variance_eps)
    inverse_a, inverse_b = 1.0 / spread_a, 1.0 / spread_b
    coef_j[0] = jnp.concatenate([local_a * inverse_a, (mean_a - center_a) * inverse_a] + [zero_row] * 6, axis=0)
    coef_z[0] = jnp.concatenate([local_b * inverse_b, (mean_b - center_b) * inverse_b] + [zero_row] * 6, axis=0)
    coef_arrive = {}
    for n, (coef, peers) in enumerate(((coef_j, j_peer), (coef_z, z_peer))):
        for r in range(1, 4):
            coef_arrive[n, r] = start(coef.at[0], coef.at[r], coef_s.at[4 * n + r], coef_r.at[4 * n + r], peers[r])

    def half_of(view, center, inverse):
        return ((view[...] - center) * inverse).astype(BF16).astype(F32)

    def rescale_a(r):
        if r:
            coef_arrive[0, r].wait_recv()
        a_buf[r, 0:ROWS] = (a_raw[r].astype(F32) * coef_j[r, 0:1] + coef_j[r, 1:2]).astype(BF16)

    def rescale_b(r):
        if r:
            coef_arrive[1, r].wait_recv()
        b_buf[r, 0:ROWS] = (b_raw[r].astype(F32) * coef_z[r, 0:1] + coef_z[r, 1:2]).astype(BF16)
        bt[r] = b_buf[r, 0:ROWS].T

    def correlate(k, m):
        block = matmul(bt[k], a_buf[m, 0:ROWS], ((1,), (0,)))
        if k == 0 and m == 0:
            same = lax.broadcasted_iota(jnp.int32, block.shape, 0) == lax.broadcasted_iota(jnp.int32, block.shape, 1)
            block = jnp.where(same, 0.0, block)
        corr[k, :, m * COLS : (m + 1) * COLS] = block
        c_send[k, :, m * COLS : (m + 1) * COLS] = block.astype(BF16)

    units = [
        (0, 0, WIDE // 2, "x"), (1, 0, WIDE, "x"), (3, 0, WIDE, "y"), (2, 0, WIDE, "x"), (0, WIDE // 2, WIDE // 2, "y"),
    ]
    right, opposite, left = (flip(across, r) for r in (1, 2, 3))
    to_right, to_left, to_mate = dp_peer[2], dp_peer[6], dp_peer[1]

    def rows_at(first, count):
        return pl.ds(pl.multiple_of(first, 16), count)

    def layout(order):
        if order == "x":
            return (lambda x: 2 * OWNED * x), 2 * OWNED
        return (lambda x: 4 * OWNED * side + OWNED * x), OWNED

    def own_rows(order, whose):
        first = 2 * OWNED * across + OWNED * whose if order == "x" else 4 * OWNED * whose + OWNED * across
        return rows_at(first, OWNED)

    near, relays, crossed = {}, {}, {}

    def send_sum(u, first, count, dst, slot, peer):
        k, c0, width, _ = units[u]
        cols = pl.ds(c0, width)
        return start(c_send.at[k, rows_at(first, count), cols], dst.at[k, :, cols], c_s.at[u, slot], c_r.at[u, slot], peer)

    def send_along_x(u):
        base, count = layout(units[u][3])
        half = count // 2
        k, c0, width, _ = units[u]
        cols = pl.ds(c0, width)

        def part(x, which, dst, slot, peer):
            return start(
                c_send.at[k, rows_at(base(x) + which * half, half), cols],
                dst.at[k, pl.ds(which * half, half), cols], c_s.at[u, slot], c_r.at[u, slot], peer,
            )

        relays[u] = [part(opposite, 0, c_relay, 0, to_right), part(opposite, 1, c_relay, 1, to_left)]
        near[u] = [part(right, 0, c_right, 2, to_right), part(left, 1, c_left, 3, to_left)]

    def relay(u):
        k, c0, width, order = units[u]
        base, count = layout(order)
        half = count // 2
        cols = slice(c0, c0 + width)
        ends = ((0, left, c_left, 4, to_left), (1, right, c_right, 5, to_right))
        for which, x, dst, slot, peer in ends:
            relays[u][which].wait_recv()
            rows = rows_at(base(x) + which * half, half)
            got = c_relay[k, which * half : (which + 1) * half, cols].astype(F32)
            c_send[k, rows, cols] = (corr[k, rows, cols] + got).astype(BF16)
            near[u].append(
                start(
                    c_send.at[k, rows, pl.ds(c0, width)], dst.at[k, pl.ds(which * half, half), pl.ds(c0, width)],
                    c_s.at[u, slot], c_r.at[u, slot], peer,
                )
            )

    def cross(u):
        k, c0, width, _ = units[u]
        rows = rows_at(4 * OWNED * (1 - side), 4 * OWNED)
        cols = pl.ds(c0, width)
        crossed[u] = start(c_send.at[k, rows, cols], c_cross.at[k, :, cols], c_s.at[u, 6], c_r.at[u, 6], to_mate)

    def cross_done(u):
        k, c0, width, _ = units[u]
        cols = slice(c0, c0 + width)
        crossed[u].wait_recv()
        rows = rows_at(4 * OWNED * side, 4 * OWNED)
        total = corr[k, rows, cols] + c_cross[k, :, cols].astype(F32)
        corr[k, rows, cols] = total
        c_send[k, rows, cols] = total.astype(BF16)
        send_along_x(u)

    weights, passed = {}, {}

    def send_weights(u, slot, rows, peer):
        k, c0, width, _ = units[u]
        part = w_buf.at[k, rows, pl.ds(c0, width)]
        return start(part, part, w_s.at[u, slot], w_r.at[u, slot], peer)

    def sum_along_x(u):
        k, c0, width, order = units[u]
        cols = slice(c0, c0 + width)
        base, count = layout(order)
        for handle in near[u]:
            handle.wait_recv()
        rows = rows_at(base(across), count)
        return (
            corr[k, rows, cols] + c_right[k, 0:count, cols].astype(F32) + c_left[k, 0:count, cols].astype(F32)
        )

    def store_weights(u, total):
        k, c0, width, order = units[u]
        w_buf[k, own_rows(order, side), c0 : c0 + width] = (total * scale_off).astype(BF16)

    def reduce_x(u):
        k, c0, width, order = units[u]
        cols = slice(c0, c0 + width)
        corr[k, rows_at(2 * OWNED * across, 2 * OWNED), cols] = sum_along_x(u)
        theirs = own_rows(order, 1 - side)
        c_send[k, theirs, cols] = corr[k, theirs, cols].astype(BF16)
        crossed[u] = start(
            c_send.at[k, theirs, pl.ds(c0, width)], c_cross.at[k, pl.ds(0, OWNED), pl.ds(c0, width)],
            c_s.at[u, 6], c_r.at[u, 6], to_mate,
        )

    def reduce_done(u):
        k, c0, width, order = units[u]
        cols = slice(c0, c0 + width)
        mine = own_rows(order, side)
        if order == "x":
            crossed[u].wait_recv()
            store_weights(u, corr[k, mine, cols] + c_cross[k, 0:OWNED, cols].astype(F32))
            weights[u] = [send_weights(u, 6, mine, to_mate)]
        else:
            store_weights(u, sum_along_x(u))
            weights[u] = []
        passed[u] = [send_weights(u, 0, mine, to_right), send_weights(u, 1, mine, to_left)]

    def pass_mate(u):
        weights[u].pop().wait_recv()
        theirs = own_rows(units[u][3], 1 - side)
        passed[u] += [send_weights(u, 2, theirs, to_right), send_weights(u, 3, theirs, to_left)]

    def pass_far(u):
        base, count = layout(units[u][3])
        half = count // 2
        for handle in passed[u]:
            handle.wait_recv()
        weights[u] += [
            send_weights(u, 4, rows_at(base(left), half), to_right),
            send_weights(u, 5, rows_at(base(right) + half, half), to_left),
        ]
        if units[u][3] == "y":
            passed[u] = [
                send_weights(u, 6 + n, rows_at(base(x), OWNED), to_mate) for n, x in enumerate((across, right, left))
            ]
        else:
            passed[u] = []

    def pass_last(u):
        for handle in weights[u]:
            handle.wait_recv()
        base, _ = layout("y")
        passed[u].append(send_weights(u, 9, rows_at(base(opposite), OWNED), to_mate))

    def gathered(u):
        for handle in passed[u] if units[u][3] == "y" else weights[u]:
            handle.wait_recv()

    rescale_a(0)
    rescale_b(0)
    correlate(0, 0)
    half_a = half_of(va, center_a, inverse_a)
    half_b = half_of(vb, center_b, inverse_b)
    shared_a = a_buf[0, 0:ROWS].astype(F32)
    shared_b = b_buf[0, 0:ROWS].astype(F32)
    mid[0] = jnp.concatenate(
        [column_sum(t) for t in (half_a * half_b, shared_a, shared_b, half_a, half_b)] + [zero_row] * 3, axis=0
    )
    mid_arrive = [start(mid.at[0], mid.at[r], mid_s.at[r], mid_r.at[r], dp_peer[r]) for r in range(1, 8)]
    a_near[1].wait_recv()
    rescale_a(1)
    correlate(0, 1)
    send_along_x(0)
    a_near[2].wait_recv()
    a_far = start(a_raw.at[2], a_raw.at[3], a_s.at[3], a_r.at[3], j_peer[1])
    b_far = []
    for r, first in ((1, 0), (3, ROWS // 2)):
        b_near[r].wait_recv()
        half = pl.ds(first, ROWS // 2)
        n = 2 if r == 1 else 0
        b_far.append(start(b_raw.at[r, half], b_raw.at[2, half], b_s.at[n], b_r.at[n], z_peer[4 - r]))
    relay(0)
    rescale_a(2)
    rescale_b(1)
    rescale_b(3)
    for k in (1, 3):
        for m in range(3):
            correlate(k, m)
    a_far.wait_recv()
    rescale_a(3)
    correlate(3, 3)
    cross(2)
    correlate(1, 3)
    send_along_x(1)
    correlate(0, 2)
    correlate(0, 3)
    cross(4)
    for handle in mid_arrive:
        handle.wait_recv()
    totals = tree_sum([mid[r] for r in range(8)])
    sums_a[0] = totals
    sums_b[0] = totals
    sum_arrive = [start(sums_a.at[0], sums_a.at[r], sum_s.at[r], sum_r.at[r], j_peer[r]) for r in range(1, 4)]
    sum_arrive += [start(sums_b.at[0], sums_b.at[r], sum_s.at[3 + r], sum_r.at[3 + r], z_peer[r]) for r in range(1, 4)]
    diagonal = totals[0:1] / BATCH
    diag_weight = (-2.0 * (1.0 - diagonal)).astype(BF16).astype(F32)
    cross_done(2)
    relay(1)
    for handle in b_far:
        handle.wait_recv()
    rescale_b(2)
    for m in range(4):
        correlate(2, m)
    send_along_x(3)
    cross_done(4)
    relay(2)
    reduce_x(1)
    relay(3)
    reduce_done(1)
    reduce_x(0)
    relay(4)
    reduce_done(2)
    pass_mate(1)
    reduce_x(3)
    pass_far(2)
    reduce_done(4)
    reduce_done(0)
    pass_far(1)
    reduce_done(3)
    pass_last(2)
    pass_far(4)
    for handle in sum_arrive:
        handle.wait_recv()
    for r in range(4):
        for sums_ref, row, buf in ((sums_a, 1, a_buf), (sums_b, 2, b_buf)):
            value = sums_ref[r, row : row + 1]
            high = value.astype(BF16)
            low = (value - high.astype(F32)).astype(BF16)
            buf[r, ROWS : ROWS + EXTRA] = jnp.concatenate(
                [high.astype(F32), low.astype(F32), jnp.zeros((EXTRA - 2, COLS), F32)], axis=0
            ).astype(BF16)
    pass_mate(3)
    pass_mate(0)

    ub_arrive = {}
    vecb_arrive = {}
    ua_done = set()

    def squares(k):
        square = jnp.square(w_buf[k].astype(F32))
        if ua_done:
            second_acc[0:1] += column_sum(square)
        else:
            second_acc[0:1] = column_sum(square)
        folded = sum(square[:, i * 128 : (i + 1) * 128] for i in range(8))
        return column_sum(folded.T)

    def upstream_of_b(k, over_first):
        total = None
        for m in range(4):
            term = matmul(a_buf[m], w_buf[k, :, m * COLS : (m + 1) * COLS], ((1,), (1,)))
            total = term if total is None else total + term
        if k == 0:
            ub_own[...] = total[0:ROWS]
        else:
            ub_send[k] = (total[0:ROWS] - b_buf[k, 0:ROWS].astype(F32) * (over_first * along)).astype(BF16)
            ub_arrive[k] = start(ub_send.at[k], ub_recv.at[k], ub_s.at[k], ub_r.at[k], z_peer[k])
        first = total[ROWS : ROWS + 1] + total[ROWS + 1 : ROWS + 2]
        slot = vec_b.at[0 if k == 0 else 3 + k]
        slot[...] = jnp.concatenate([first, over_first] + [zero_row] * 6, axis=0)
        if k:
            vecb_arrive[k] = start(slot, vec_b.at[k], vec_s.at[3 + k], vec_r.at[3 + k], z_peer[k])

    def upstream_of_a(k, m):
        term = matmul(b_buf[k], w_buf[k, :, m * COLS : (m + 1) * COLS], ((1,), (0,)))
        if m in ua_done:
            ua_acc[m] += term
        else:
            ua_acc[m] = term
            ua_done.add(m)

    def take_out(r):
        taken = second_acc[0:1, r * COLS : (r + 1) * COLS] * along
        ua_acc[r, 0:ROWS] -= a_buf[r, 0:ROWS].astype(F32) * taken

    gathered(1)
    over_first = squares(1)
    upstream_of_b(1, over_first)
    for m in range(4):
        upstream_of_a(1, m)
    pass_far(3)
    pass_far(0)
    pass_last(4)
    gathered(2)
    over_first = squares(3)
    upstream_of_b(3, over_first)
    for m in range(4):
        upstream_of_a(3, m)
    gathered(3)
    over_first = squares(2)
    upstream_of_b(2, over_first)
    for m in range(4):
        upstream_of_a(2, m)
    gathered(0)
    gathered(4)
    over_first = squares(0)
    upstream_of_a(0, 3)
    take_out(3)
    ua3 = start(ua_acc.at[3, pl.ds(0, ROWS)], ua_near.at[1], ua_s.at[3], ua_r.at[3], j_peer[1])
    upstream_of_a(0, 2)
    take_out(2)
    ua3.wait_recv()
    ua_send[...] = (ua_acc[2, 0:ROWS] + ua_near[1]).astype(BF16)
    ua2 = start(ua_send, ua_recv, ua_s.at[2], ua_r.at[2], j_peer[2])
    upstream_of_a(0, 1)
    ua1 = start(ua_acc.at[1, pl.ds(0, ROWS)], ua_near.at[0], ua_s.at[1], ua_r.at[1], j_peer[1])
    upstream_of_a(0, 0)
    upstream_of_b(0, over_first)

    block_sum = sum(second_acc[0:1, m * COLS : (m + 1) * COLS] for m in range(4))
    loss_row = (1.0 - diagonal) ** 2 + (0.25 / off_weight) * block_sum
    vec_arrive = []
    for r in range(4):
        first = ua_acc[r, ROWS : ROWS + 1] + ua_acc[r, ROWS + 1 : ROWS + 2]
        second = second_acc[0:1, r * COLS : (r + 1) * COLS]
        slot = vec_a.at[0 if r == 0 else 3 + r]
        slot[...] = jnp.concatenate([first, second, loss_row] + [zero_row] * 5, axis=0)
        if r:
            vec_arrive.append(start(slot, vec_a.at[r], vec_s.at[r], vec_r.at[r], j_peer[r]))
    for handle in vec_arrive:
        handle.wait_recv()
    sum_a = tree_sum([vec_a[r] for r in range(4)])
    vec_l[0] = sum_a
    loss_arrive = [start(vec_l.at[0], vec_l.at[r], vl_s.at[r], vl_r.at[r], z_peer[r]) for r in range(1, 4)]
    for handle in vecb_arrive.values():
        handle.wait_recv()
    sum_b = tree_sum([vec_b[r] for r in range(4)])
    for handle in loss_arrive:
        handle.wait_recv()
    losses = tree_sum([vec_l[r] for r in range(4)])
    loss[...] = jnp.sum(losses[2:3], axis=1, keepdims=True) / D

    def finish(upstream, view, center, inverse, own_sum, sums, out):
        first = (sums[0:1] + diag_weight * own_sum) / BATCH
        second = sums[1:2] * along + diag_weight * diagonal
        normed = (view[...] - center) * inverse
        out[...] = (upstream - first - normed * second) * inverse

    for k in (1, 3, 2):
        ub_arrive[k].wait_recv()
    upstream_b = ub_own[...] + sum(ub_recv[k].astype(F32) for k in (1, 2, 3)) + diag_weight * half_of(va, center_a, inverse_a)
    taken = (vec_b[1, 1:2] + vec_b[2, 1:2] + vec_b[3, 1:2]) * along
    upstream_b = upstream_b + taken * b_buf[0, 0:ROWS].astype(F32)
    finish(upstream_b, vb, center_b, inverse_b, totals[3:4], sum_b, gb)
    ua1.wait_recv()
    taken = (vec_a[2, 1:2] + vec_a[3, 1:2]) * along
    upstream_a = ua_acc[0, 0:ROWS] + ua_near[0] + diag_weight * half_of(vb, center_b, inverse_b)
    upstream_a = upstream_a + taken * a_buf[0, 0:ROWS].astype(F32)
    finish(upstream_a, va, center_a, inverse_a, totals[4:5], sum_a, ga)
    for handle in pending:
        if handle is not ua2:
            handle.wait_send()
    ua2.wait_recv()
    ga[...] += ua_recv[...].astype(F32) * inverse_a
    ua2.wait_send()


def per_device(view_a, view_b):
    view = VMEM((ROWS, COLS), F32)
    small = VMEM((8, 8, COLS), F32)
    block = VMEM((4, ROWS + EXTRA, COLS), BF16)
    plain = VMEM((4, ROWS, COLS), BF16)
    chunk = (4, COLS, WIDE)
    pair = VMEM((4, 2 * OWNED, WIDE), BF16)
    grad_a, grad_b, loss = pl.pallas_call(
        kernel,
        out_shape=(
            jax.ShapeDtypeStruct((ROWS, COLS), F32),
            jax.ShapeDtypeStruct((ROWS, COLS), F32),
            jax.ShapeDtypeStruct((1, 1), F32),
        ),
        in_specs=[pl.BlockSpec(memory_space=pltpu.HBM)] * 2,
        out_specs=[pl.BlockSpec(memory_space=VMEM)] * 3,
        scratch_shapes=[
            view, view, small, small, small, small, small, small, small,
            VMEM((4, 8, COLS), F32), VMEM((4, 8, COLS), F32), plain, plain, block, block, VMEM((4, COLS, ROWS), BF16), VMEM(chunk, F32), VMEM(chunk, BF16), pair, pair, pair, VMEM((4, 4 * OWNED, WIDE), BF16),
            VMEM(chunk, BF16),
            VMEM((4, ROWS + EXTRA, COLS), F32), VMEM((ROWS, COLS), F32),
            VMEM((2, ROWS, COLS), F32), VMEM((ROWS, COLS), BF16), VMEM((ROWS, COLS), BF16), plain, plain, VMEM((8, WIDE), F32),
            DMA((2,)), *[DMA((8,))] * 12, *[DMA((4,))] * 4, *[DMA((5, 10))] * 4, *[DMA((4,))] * 4,
        ],
        compiler_params=pltpu.CompilerParams(
            collective_id=0, has_side_effects=True, vmem_limit_bytes=44 * 1024 * 1024
        ),
        cost_estimate=pl.CostEstimate(flops=3 * 2 * 1024**3, bytes_accessed=4 * 1024 * 1024, transcendentals=0),
        name="twins",
    )(view_a, view_b)
    return grad_a, grad_b, loss[0, 0]


def solution(mesh):
    in_specs = (P("dp", "feat"), P("dp", "feat"))
    out_specs = (P("dp", "feat"), P("dp", "feat"), P())
    return jax.shard_map(
        per_device, mesh=mesh, in_specs=in_specs, out_specs=out_specs, check_vma=False
    )
```

time: 109 us -> 96.4 us (0.88); the launches traced: 107 us -> 96.2 us
  Pallas kernels: 101 us -> 89.4 us
    pallas_call x1, Pallas kernels: 101 us -> 89.4 us  [per_device(): pl.pallas_call(kernel, out_shape=(jax.ShapeDtypeStruct((ROWS, COLS), F32)...]
    unnamed x4 -> x6, local copies, waits for them, and re-layouts: 3.32 us -> 4.38 us
where the time goes in v2:
time: 96.4 us; the launch traced here: 96.2 us
  Pallas kernels  89.4 us (93%)
  local copies, waits for them, and re-layouts  4.38 us (5%)
  between operations  2.41 us (2%)
    pallas_call x1, Pallas kernels, per_device(): pl.pallas_call(kernel, out_shape=(jax.ShapeDtypeStruct((ROWS, COLS), F32)...  89.4 us
    unnamed x6, local copies, waits for them, and re-layouts  4.38 us

profile of v2, /device:TPU:0, one launch (start us, length us, event | category | flops | bytes accessed | tf_op | source)
XLA Modules:
  0.0 96.2 jit_solution(5503230476391271436)
XLA Ops:
  0.6 0.0 copy-start
  0.6 1.2 %copy-done = f32[1024,256]{1,0:T(8,128)S(1)} copy-done((f32[1024,256]{1,0:T(8,128)S(1)}, f32[1024,256]{1,0:T(8,128)}, u32[]{:S(2)}) %copy-start) | copy-done | bytes 1048600
  1.9 0.0 copy-start.1
  1.9 1.2 %copy-done.1 = f32[1024,256]{1,0:T(8,128)S(1)} copy-done((f32[1024,256]{1,0:T(8,128)S(1)}, f32[1024,256]{1,0:T(8,128)}, u32[]{:S(2)}) %copy-start.1) | copy-done | bytes 1048600
  3.1 89.4 %twins.1 = (f32[1024,256]{1,0:T(8,128)S(1)}, f32[1024,256]{1,0:T(8,128)S(1)}, f32[1,1]{1,0:T(1,128)}) custom-call(f32[1024,256]{1,0:T(8,128)S(1)} %copy-done, f32[1024,256]{1,0:T(8,128)S(1)} %copy-done.1), custom_call_target="tpu_custom_call" | custom-call | flops 6442450944 | bytes 4194304 | tf_op jit(solution)/shard_map/twins/pallas_call | solution.py:509
  92.5 1.0 %copy.8 = f32[1024,256]{1,0:T(8,128)} copy(f32[1024,256]{1,0:T(8,128)S(1)} %get-tuple-element.12) | data formatting | bytes 2097152
  93.5 1.0 %copy.9 = f32[1024,256]{1,0:T(8,128)} copy(f32[1024,256]{1,0:T(8,128)S(1)} %get-tuple-element.13) | data formatting | bytes 2097152
Async XLA Ops:
  0.6 1.2 %copy-start = (f32[1024,256]{1,0:T(8,128)S(1)}, f32[1024,256]{1,0:T(8,128)}, u32[]{:S(2)}) copy-start(f32[1024,256]{1,0:T(8,128)} %va_hbm.1) | copy-start | bytes 3145732
  1.9 1.2 %copy-start.1 = (f32[1024,256]{1,0:T(8,128)S(1)}, f32[1024,256]{1,0:T(8,128)}, u32[]{:S(2)}) copy-start(f32[1024,256]{1,0:T(8,128)} %vb_hbm.1) | copy-start | bytes 3145732

commit v3 on v2

--- a/solution.py
+++ b/solution.py
@@ -293,14 +293,6 @@
     rescale_a(0)
     rescale_b(0)
     correlate(0, 0)
-    half_a = half_of(va, center_a, inverse_a)
-    half_b = half_of(vb, center_b, inverse_b)
-    shared_a = a_buf[0, 0:ROWS].astype(F32)
-    shared_b = b_buf[0, 0:ROWS].astype(F32)
-    mid[0] = jnp.concatenate(
-        [column_sum(t) for t in (half_a * half_b, shared_a, shared_b, half_a, half_b)] + [zero_row] * 3, axis=0
-    )
-    mid_arrive = [start(mid.at[0], mid.at[r], mid_s.at[r], mid_r.at[r], dp_peer[r]) for r in range(1, 8)]
     a_near[1].wait_recv()
     rescale_a(1)
     correlate(0, 1)
@@ -329,6 +321,25 @@
     correlate(0, 2)
     correlate(0, 3)
     cross(4)
+    half_a = half_of(va, center_a, inverse_a)
+    half_b = half_of(vb, center_b, inverse_b)
+    shared_a = a_buf[0, 0:ROWS].astype(F32)
+    shared_b = b_buf[0, 0:ROWS].astype(F32)
+    mid[0] = jnp.concatenate(
+        [column_sum(t) for t in (half_a * half_b, shared_a, shared_b, half_a, half_b)] + [zero_row] * 3, axis=0
+    )
+    mid_arrive = [start(mid.at[0], mid.at[r], mid_s.at[r], mid_r.at[r], dp_peer[r]) for r in range(1, 8)]
+    cross_done(2)
+    relay(1)
+    for handle in b_far:
+        handle.wait_recv()
+    rescale_b(2)
+    for m in range(4):
+        correlate(2, m)
+    send_along_x(3)
+    cross_done(4)
+    relay(2)
+    reduce_x(1)
     for handle in mid_arrive:
         handle.wait_recv()
     totals = tree_sum([mid[r] for r in range(8)])
@@ -338,17 +349,6 @@
     sum_arrive += [start(sums_b.at[0], sums_b.at[r], sum_s.at[3 + r], sum_r.at[3 + r], z_peer[r]) for r in range(1, 4)]
     diagonal = totals[0:1] / BATCH
     diag_weight = (-2.0 * (1.0 - diagonal)).astype(BF16).astype(F32)
-    cross_done(2)
-    relay(1)
-    for handle in b_far:
-        handle.wait_recv()
-    rescale_b(2)
-    for m in range(4):
-        correlate(2, m)
-    send_along_x(3)
-    cross_done(4)
-    relay(2)
-    reduce_x(1)
     relay(3)
     reduce_done(1)
     reduce_x(0)
@@ -394,16 +394,16 @@
         for m in range(4):
             term = matmul(a_buf[m], w_buf[k, :, m * COLS : (m + 1) * COLS], ((1,), (1,)))
             total = term if total is None else total + term
+        first = total[ROWS : ROWS + 1] + total[ROWS + 1 : ROWS + 2]
+        slot = vec_b.at[0 if k == 0 else 3 + k]
+        slot[...] = jnp.concatenate([first, over_first] + [zero_row] * 6, axis=0)
+        if k:
+            vecb_arrive[k] = start(slot, vec_b.at[k], vec_s.at[3 + k], vec_r.at[3 + k], z_peer[k])
         if k == 0:
             ub_own[...] = total[0:ROWS]
         else:
             ub_send[k] = (total[0:ROWS] - b_buf[k, 0:ROWS].astype(F32) * (over_first * along)).astype(BF16)
             ub_arrive[k] = start(ub_send.at[k], ub_recv.at[k], ub_s.at[k], ub_r.at[k], z_peer[k])
-        first = total[ROWS : ROWS + 1] + total[ROWS + 1 : ROWS + 2]
-        slot = vec_b.at[0 if k == 0 else 3 + k]
-        slot[...] = jnp.concatenate([first, over_first] + [zero_row] * 6, axis=0)
-        if k:
-            vecb_arrive[k] = start(slot, vec_b.at[k], vec_s.at[3 + k], vec_r.at[3 + k], z_peer[k])
 
     def upstream_of_a(k, m):
         term = matmul(b_buf[k], w_buf[k, :, m * COLS : (m + 1) * COLS], ((1,), (0,)))
@@ -438,18 +438,13 @@
     gathered(0)
     gathered(4)
     over_first = squares(0)
-    upstream_of_a(0, 3)
-    take_out(3)
-    ua3 = start(ua_acc.at[3, pl.ds(0, ROWS)], ua_near.at[1], ua_s.at[3], ua_r.at[3], j_peer[1])
-    upstream_of_a(0, 2)
+    for m in (3, 1, 2, 0):
+        upstream_of_a(0, m)
+        if m == 3:
+            take_out(3)
+            ua3 = start(ua_acc.at[3, pl.ds(0, ROWS)], ua_near.at[1], ua_s.at[3], ua_r.at[3], j_peer[1])
+    ua1 = start(ua_acc.at[1, pl.ds(0, ROWS)], ua_near.at[0], ua_s.at[1], ua_r.at[1], j_peer[1])
     take_out(2)
-    ua3.wait_recv()
-    ua_send[...] = (ua_acc[2, 0:ROWS] + ua_near[1]).astype(BF16)
-    ua2 = start(ua_send, ua_recv, ua_s.at[2], ua_r.at[2], j_peer[2])
-    upstream_of_a(0, 1)
-    ua1 = start(ua_acc.at[1, pl.ds(0, ROWS)], ua_near.at[0], ua_s.at[1], ua_r.at[1], j_peer[1])
-    upstream_of_a(0, 0)
-    upstream_of_b(0, over_first)
 
     block_sum = sum(second_acc[0:1, m * COLS : (m + 1) * COLS] for m in range(4))
     loss_row = (1.0 - diagonal) ** 2 + (0.25 / off_weight) * block_sum
@@ -461,6 +456,10 @@
         slot[...] = jnp.concatenate([first, second, loss_row] + [zero_row] * 5, axis=0)
         if r:
             vec_arrive.append(start(slot, vec_a.at[r], vec_s.at[r], vec_r.at[r], j_peer[r]))
+    ua3.wait_recv()
+    ua_send[...] = (ua_acc[2, 0:ROWS] + ua_near[1]).astype(BF16)
+    ua2 = start(ua_send, ua_recv, ua_s.at[2], ua_r.at[2], j_peer[2])
+    upstream_of_b(0, over_first)
     for handle in vec_arrive:
         handle.wait_recv()
     sum_a = tree_sum([vec_a[r] for r in range(4)])
@@ -469,11 +468,6 @@
     for handle in vecb_arrive.values():
         handle.wait_recv()
     sum_b = tree_sum([vec_b[r] for r in range(4)])
-    for handle in loss_arrive:
-        handle.wait_recv()
-    losses = tree_sum([vec_l[r] for r in range(4)])
-    loss[...] = jnp.sum(losses[2:3], axis=1, keepdims=True) / D
-
     def finish(upstream, view, center, inverse, own_sum, sums, out):
         first = (sums[0:1] + diag_weight * own_sum) / BATCH
         second = sums[1:2] * along + diag_weight * diagonal
@@ -491,6 +485,10 @@
     upstream_a = ua_acc[0, 0:ROWS] + ua_near[0] + diag_weight * half_of(vb, center_b, inverse_b)
     upstream_a = upstream_a + taken * a_buf[0, 0:ROWS].astype(F32)
     finish(upstream_a, va, center_a, inverse_a, totals[4:5], sum_a, ga)
+    for handle in loss_arrive:
+        handle.wait_recv()
+    losses = tree_sum([vec_l[r] for r in range(4)])
+    loss[...] = jnp.sum(losses[2:3], axis=1, keepdims=True) / D
     for handle in pending:
         if handle is not ua2:
             handle.wait_send()

time: 96.4 us -> 94.1 us (0.976)
  Pallas kernels: 89.4 us -> 87.1 us
    pallas_call x1, Pallas kernels: 89.4 us -> 87.1 us  [per_device(): pl.pallas_call(kernel, out_shape=(jax.ShapeDtypeStruct((ROWS, COLS), F32)...]
where the time goes in v3:
time: 94.1 us; the launch traced here: 93.9 us
  Pallas kernels  87.1 us (93%)
  local copies, waits for them, and re-layouts  4.38 us (5%)
  between operations  2.41 us (3%)
    pallas_call x1, Pallas kernels, per_device(): pl.pallas_call(kernel, out_shape=(jax.ShapeDtypeStruct((ROWS, COLS), F32)...  87.1 us
    unnamed x6, local copies, waits for them, and re-layouts  4.38 us

profile of v3, /device:TPU:0, one launch (start us, length us, event | category | flops | bytes accessed | tf_op | source)
XLA Modules:
  0.0 93.9 jit_solution(15809935811820791605)
XLA Ops:
  0.6 0.0 copy-start
  0.6 1.2 %copy-done = f32[1024,256]{1,0:T(8,128)S(1)} copy-done((f32[1024,256]{1,0:T(8,128)S(1)}, f32[1024,256]{1,0:T(8,128)}, u32[]{:S(2)}) %copy-start) | copy-done | bytes 1048600
  1.9 0.0 copy-start.1
  1.9 1.2 %copy-done.1 = f32[1024,256]{1,0:T(8,128)S(1)} copy-done((f32[1024,256]{1,0:T(8,128)S(1)}, f32[1024,256]{1,0:T(8,128)}, u32[]{:S(2)}) %copy-start.1) | copy-done | bytes 1048600
  3.1 87.1 %twins.1 = (f32[1024,256]{1,0:T(8,128)S(1)}, f32[1024,256]{1,0:T(8,128)S(1)}, f32[1,1]{1,0:T(1,128)}) custom-call(f32[1024,256]{1,0:T(8,128)S(1)} %copy-done, f32[1024,256]{1,0:T(8,128)S(1)} %copy-done.1), custom_call_target="tpu_custom_call" | custom-call | flops 6442450944 | bytes 4194304 | tf_op jit(solution)/shard_map/twins/pallas_call | solution.py:507
  90.2 1.0 %copy.8 = f32[1024,256]{1,0:T(8,128)} copy(f32[1024,256]{1,0:T(8,128)S(1)} %get-tuple-element.12) | data formatting | bytes 2097152
  91.2 1.0 %copy.9 = f32[1024,256]{1,0:T(8,128)} copy(f32[1024,256]{1,0:T(8,128)S(1)} %get-tuple-element.13) | data formatting | bytes 2097152
Async XLA Ops:
  0.6 1.2 %copy-start = (f32[1024,256]{1,0:T(8,128)S(1)}, f32[1024,256]{1,0:T(8,128)}, u32[]{:S(2)}) copy-start(f32[1024,256]{1,0:T(8,128)} %va_hbm.1) | copy-start | bytes 3145732
  1.9 1.2 %copy-start.1 = (f32[1024,256]{1,0:T(8,128)S(1)}, f32[1024,256]{1,0:T(8,128)}, u32[]{:S(2)}) copy-start(f32[1024,256]{1,0:T(8,128)} %vb_hbm.1) | copy-start | bytes 3145732

commit v4 on v3

--- a/solution.py
+++ b/solution.py
@@ -474,17 +474,18 @@
         normed = (view[...] - center) * inverse
         out[...] = (upstream - first - normed * second) * inverse
 
-    for k in (1, 3, 2):
-        ub_arrive[k].wait_recv()
-    upstream_b = ub_own[...] + sum(ub_recv[k].astype(F32) for k in (1, 2, 3)) + diag_weight * half_of(va, center_a, inverse_a)
-    taken = (vec_b[1, 1:2] + vec_b[2, 1:2] + vec_b[3, 1:2]) * along
-    upstream_b = upstream_b + taken * b_buf[0, 0:ROWS].astype(F32)
-    finish(upstream_b, vb, center_b, inverse_b, totals[3:4], sum_b, gb)
     ua1.wait_recv()
     taken = (vec_a[2, 1:2] + vec_a[3, 1:2]) * along
     upstream_a = ua_acc[0, 0:ROWS] + ua_near[0] + diag_weight * half_of(vb, center_b, inverse_b)
     upstream_a = upstream_a + taken * a_buf[0, 0:ROWS].astype(F32)
     finish(upstream_a, va, center_a, inverse_a, totals[4:5], sum_a, ga)
+    upstream_b = ub_own[...] + diag_weight * half_of(va, center_a, inverse_a)
+    taken = (vec_b[1, 1:2] + vec_b[2, 1:2] + vec_b[3, 1:2]) * along
+    upstream_b = upstream_b + taken * b_buf[0, 0:ROWS].astype(F32)
+    finish(upstream_b, vb, center_b, inverse_b, totals[3:4], sum_b, gb)
+    for k in (1, 3, 2):
+        ub_arrive[k].wait_recv()
+    gb[...] += sum(ub_recv[k].astype(F32) for k in (1, 2, 3)) * inverse_b
     for handle in loss_arrive:
         handle.wait_recv()
     losses = tree_sum([vec_l[r] for r in range(4)])

time: 94.1 us -> 93.1 us (0.989)
  Pallas kernels: 87.1 us -> 86.1 us
    pallas_call x1, Pallas kernels: 87.1 us -> 86.1 us  [per_device(): pl.pallas_call(kernel, out_shape=(jax.ShapeDtypeStruct((ROWS, COLS), F32)...]
where the time goes in v4:
time: 93.1 us; the launch traced here: 92.9 us
  Pallas kernels  86.1 us (92%)
  local copies, waits for them, and re-layouts  4.38 us (5%)
  between operations  2.41 us (3%)
    pallas_call x1, Pallas kernels, per_device(): pl.pallas_call(kernel, out_shape=(jax.ShapeDtypeStruct((ROWS, COLS), F32)...  86.1 us
    unnamed x6, local copies, waits for them, and re-layouts  4.38 us

profile of v4, /device:TPU:0, one launch (start us, length us, event | category | flops | bytes accessed | tf_op | source)
XLA Modules:
  0.0 92.9 jit_solution(4582372717864391243)
XLA Ops:
  0.6 0.0 copy-start
  0.6 1.2 %copy-done = f32[1024,256]{1,0:T(8,128)S(1)} copy-done((f32[1024,256]{1,0:T(8,128)S(1)}, f32[1024,256]{1,0:T(8,128)}, u32[]{:S(2)}) %copy-start) | copy-done | bytes 1048600
  1.9 0.0 copy-start.1
  1.9 1.2 %copy-done.1 = f32[1024,256]{1,0:T(8,128)S(1)} copy-done((f32[1024,256]{1,0:T(8,128)S(1)}, f32[1024,256]{1,0:T(8,128)}, u32[]{:S(2)}) %copy-start.1) | copy-done | bytes 1048600
  3.1 86.1 %twins.1 = (f32[1024,256]{1,0:T(8,128)S(1)}, f32[1024,256]{1,0:T(8,128)S(1)}, f32[1,1]{1,0:T(1,128)}) custom-call(f32[1024,256]{1,0:T(8,128)S(1)} %copy-done, f32[1024,256]{1,0:T(8,128)S(1)} %copy-done.1), custom_call_target="tpu_custom_call" | custom-call | flops 6442450944 | bytes 4194304 | tf_op jit(solution)/shard_map/twins/pallas_call | solution.py:508
  89.2 1.0 %copy.8 = f32[1024,256]{1,0:T(8,128)} copy(f32[1024,256]{1,0:T(8,128)S(1)} %get-tuple-element.12) | data formatting | bytes 2097152
  90.2 1.0 %copy.9 = f32[1024,256]{1,0:T(8,128)} copy(f32[1024,256]{1,0:T(8,128)S(1)} %get-tuple-element.13) | data formatting | bytes 2097152
Async XLA Ops:
  0.6 1.2 %copy-start = (f32[1024,256]{1,0:T(8,128)S(1)}, f32[1024,256]{1,0:T(8,128)}, u32[]{:S(2)}) copy-start(f32[1024,256]{1,0:T(8,128)} %va_hbm.1) | copy-start | bytes 3145732
  1.9 1.2 %copy-start.1 = (f32[1024,256]{1,0:T(8,128)S(1)}, f32[1024,256]{1,0:T(8,128)}, u32[]{:S(2)}) copy-start(f32[1024,256]{1,0:T(8,128)} %vb_hbm.1) | copy-start | bytes 3145732
